TPU v7x, 32 devices: a whole 2x2x4 slice. The times are simulated.
32 devices in a mesh: tile: 8 (over y, x, core), spec: 4 (over z).
Axes of the slice: x: 2, y: 2, z: 4, core: 2. Of those that a mesh axis runs over, the one named last changes fastest.
Arguments:
- concentrations: float32 [32, 512, 256], P('spec', 'tile'), may hold values from 0.1 to 4
- courant: float32 [512, 256], P('tile'), may hold values from 0.05 to 0.95
- first_weight: bfloat16 [32, 512], replicated, may hold values from -1 to 1
- middle_weight: bfloat16 [512, 512], replicated, may hold values from -0.25 to 0.25
- last_weight: bfloat16 [512, 32], replicated, may hold values from -0.25 to 0.25
- active_blocks: int32 [8, 4, 16], P('tile', 'spec'), may hold values from 0 to 32, as said below
- dest_tile: int32 [8, 4, 16], P('tile', 'spec'), may hold values from 0 to 7, as said below
Outputs:
- chemistry_out: bfloat16 [32, 131072], P(None, ('tile', 'spec'))
- load_share: float32 [8, 4], P('tile', 'spec')
Inputs may be any that keep to these rules, and one draw needn't show every extreme that they name: `active_blocks`: each device's entries name distinct blocks of its own 32; the value 32 marks an empty slot. `dest_tile`: A listed block's tile lies within 2 tiles of its home tile along the periodic order of tiles; an empty slot names the home tile. At most 2 blocks of one device name one other tile, and at most 8 listed blocks over all devices of one spec index name one tile; both bounds are reached in every draw.
All inputs are finite; a program needn't handle non-finite values.
Results may differ from a plain program's by a relative error of at most 0.0035.
Values may be sent and summed in bfloat16 or wider, within the bound.
No kernel may reach another device: no remote copies, remote signals or barrier semaphores. Data moves between devices by JAX's collectives and lax.ppermute only.
A program may use at most 64 MiB of HBM per device.

v0:
```python
import functools

import jax
import jax.numpy as jnp
from jax import lax
from jax.experimental import pallas as pl
from jax.experimental.pallas import tpu as pltpu
from jax.sharding import PartitionSpec as P

BLK = 128
RECV = 8
LANES = 128
SUB = 8
EACH = 4
BEHIND = 4
AHEAD = 2
VMEM_BYTES = 16 * 1024 * 1024


def silu_of_half(half):
    return half + half * jnp.tanh(half)


def sweep_rows(rows, rates):
    diffs = [b - a for a, b in zip(rows[:-1], rows[1:])]
    fluxes = []
    for at in range(1, len(rows) - 1):
        left, right = diffs[at - 1], diffs[at]
        slope = jnp.maximum(jnp.minimum(left, right), 0.0) + jnp.minimum(
            jnp.maximum(left, right), 0.0
        )
        rate, damp = rates[at]
        fluxes.append(rate * (rows[at] + damp * slope))
    return [rows[at] - fluxes[at - 1] + fluxes[at - 2] for at in range(2, len(rows) - 1)]


def two_sweeps(rows, rates):
    once = sweep_rows(rows, rates)
    return sweep_rows(once, rates[2:-1])


def with_damp(rate, shape):
    rate = jnp.broadcast_to(rate, shape)
    return rate, 0.5 - 0.5 * rate


def tiled(x, halves):
    lead, (rows, cols) = x.shape[:-2], x.shape[-2:]
    x = x.reshape(lead + (rows // SUB, SUB, halves, LANES))
    axes = tuple(range(len(lead)))
    x = x.transpose(axes + tuple(len(lead) + a for a in (0, 2, 1, 3)))
    return x.reshape(lead + (rows * halves, LANES))


def spot(at, half, halves):
    return (at // SUB * halves + half) * SUB + at % SUB


def pack_kernel(
    length, halves, blocks, q_in, rates_in, list_in, dest_in, row_in,
    even_ref, odd_ref, hits_ref, row_ref, low_ref, high_ref, rates_ref, list_ref, dest_ref, arrived,
):
    species, rows = q_in.shape[:2]
    tile = halves * SUB
    part = BEHIND * species + SUB
    shape = (species, tile, LANES)
    pairs = [
        (q_in.at[:, rows - tile :], high_ref.reshape(shape)),
        (q_in.at[:, :tile], low_ref.reshape(shape)),
        (rates_in.at[rows - tile :], rates_ref.at[tile:]),
        (rates_in.at[:tile], rates_ref.at[:tile]),
        (list_in, list_ref),
        (dest_in, dest_ref),
        (row_in, row_ref),
    ]
    copies = [
        pltpu.make_async_copy(source, target, arrived.at[i])
        for i, (source, target) in enumerate(pairs)
    ]
    for copy in copies:
        copy.start()
    copies[4].wait()
    copies[5].wait()
    lane = lax.broadcasted_iota(jnp.int32, (SUB, LANES), 1)
    hits = jnp.zeros((SUB, LANES), jnp.float32)
    for j in range(list_ref.shape[0]):
        target = jnp.where(list_ref[j] < blocks, dest_ref[j], -1)
        hits = hits + jnp.where(lane == target, 1.0, 0.0)
    hits_ref[...] = hits
    for copy in copies[:4] + copies[6:]:
        copy.wait()

    def write(up_ref, down_ref):
        for half in range(halves):
            start = half * part
            for j in range(BEHIND):
                at = start + j * species
                up_ref[at : at + species, :] = high_ref[
                    pl.ds(half * SUB + SUB - BEHIND + j, species, stride=tile), :
                ]
                if j < AHEAD:
                    value = low_ref[pl.ds(half * SUB + j, species, stride=tile), :]
                else:
                    value = jnp.zeros((species, LANES), jnp.float32)
                down_ref[at : at + species, :] = value
            at = start + BEHIND * species
            up_ref[at : at + SUB, :] = rates_ref[tile + half * SUB : tile + (half + 1) * SUB, :]
            down_ref[at : at + SUB, :] = rates_ref[half * SUB : (half + 1) * SUB, :]
        up_ref[halves * part :, :] = hits
        down_ref[halves * part :, :] = hits

    even = lax.rem(lax.axis_index("tile"), 2) == 0

    @pl.when(even)
    def _():
        write(even_ref, odd_ref)

    @pl.when(jnp.logical_not(even))
    def _():
        write(odd_ref, even_ref)


def inner_kernel(dests, length, halves, q_ref, rates_ref, *out_refs):
    species = out_refs[0].shape[0]
    share = length // dests
    me = lax.axis_index("spec")
    for k in range(dests):
        first = lax.rem(me + k, dests) * share
        below = jnp.maximum(first - SUB, 0)
        above = jnp.minimum(first + share, length - SUB)
        for half in range(halves):

            def start(at):
                if at < 0:
                    return below * halves + spot(at + SUB, half, halves)
                if at >= share:
                    return above * halves + spot(at - share, half, halves)
                return first * halves + spot(at, half, halves)

            reach = range(-BEHIND, share + AHEAD)
            rows = [q_ref[pl.ds(start(at), species, stride=length * halves), :] for at in reach]
            rates = [
                with_damp(rates_ref[pl.ds(start(at), 1), :], (species, LANES)) for at in reach
            ]
            for at, value in enumerate(two_sweeps(rows, rates)):
                place = (at * halves + half) * LANES
                out_refs[k][:, place : place + LANES] = value.astype(jnp.bfloat16)


def edge_kernel(
    dests, length, halves, odd_ref, even_ref, hits_ref, q_ref, rates_ref, *refs
):
    in_refs, out_refs, (to_even_ref, to_odd_ref, known_ref) = (
        refs[:dests], refs[dests : 2 * dests], refs[2 * dests :]
    )
    species, cells = out_refs[0].shape
    me = lax.axis_index("spec")
    part = BEHIND * species + SUB
    reach = BEHIND + AHEAD
    even = lax.rem(lax.axis_index("tile"), 2) == 0
    own, from_even, from_odd = hits_ref[...], even_ref[halves * part :, :], odd_ref[halves * part :, :]
    known_ref[...] = own + from_even + from_odd
    to_even_ref[...] = from_odd
    to_odd_ref[...] = from_even

    def message(behind, at, size):
        a, b = odd_ref[at : at + size, :], even_ref[at : at + size, :]
        return jnp.where(even, a, b) if behind else jnp.where(even, b, a)

    def row(at, half):
        return q_ref[pl.ds(spot(at, half, halves), species, stride=length * halves), :]

    def rates_of(values):
        return [with_damp(value, (species, LANES)) for value in values]

    tops, bottoms = [], []
    for half in range(halves):
        base = half * part
        behind = [message(True, base + j * species, species) for j in range(BEHIND)]
        ahead = [message(False, base + j * species, species) for j in range(AHEAD)]
        before = message(True, base + BEHIND * species, SUB)
        after = message(False, base + BEHIND * species, SUB)

        def own_rates(first):
            places = [spot(first + j, half, halves) for j in range(reach)]
            return [rates_ref[at : at + 1, :] for at in places]

        tops.append(
            two_sweeps(
                behind + [row(j, half) for j in range(reach)],
                rates_of([before[SUB - BEHIND + j :][:1] for j in range(BEHIND)] + own_rates(0)),
            )
        )
        bottoms.append(
            two_sweeps(
                [row(length - reach + j, half) for j in range(reach)] + ahead,
                rates_of(own_rates(length - reach) + [after[j : j + 1] for j in range(AHEAD)]),
            )
        )
    for k, (in_ref, out_ref) in enumerate(zip(in_refs, out_refs)):
        dest = lax.rem(me + k, dests)
        out_ref[...] = in_ref[...]

        @pl.when(dest == 0)
        def _():
            for half in range(halves):
                for j, value in enumerate(tops[half]):
                    at = (j * halves + half) * LANES
                    out_ref[:, at : at + LANES] = value.astype(jnp.bfloat16)

        @pl.when(dest == dests - 1)
        def _():
            for half in range(halves):
                for j, value in enumerate(bottoms[half]):
                    at = cells + ((j - AHEAD) * halves + half) * LANES
                    out_ref[:, at : at + LANES] = value.astype(jnp.bfloat16)


def weight_kernel(w1_ref, w2_ref, after_ref, w1_out, w2_out):
    w1_out[...] = (0.5 * w1_ref[...].astype(jnp.float32)).T.astype(jnp.bfloat16)
    w2_out[...] = (0.5 * w2_ref[...].astype(jnp.float32)).T.astype(jnp.bfloat16)


def chemistry_kernel(
    groups, named_in, w1_ref, w2_ref, w3_ref, *refs
):
    parts, (known_ref, odd_ref, even_ref), refs = (
        refs[:groups], refs[groups : groups + 3], refs[groups + 3 :]
    )
    out_ref, share_ref, named_ref, list_ref, picked_ref, fresh_ref, held_ref, done = refs
    listing = pltpu.make_async_copy(named_in, named_ref, done.at[groups + 1])
    listing.start()
    species, cells = parts[0].shape
    slots = named_ref.shape[1]
    blocks = cells // BLK
    me = lax.axis_index("spec")
    sources = [lax.rem(me - k + groups, groups) for k in range(groups)]
    copies = [
        pltpu.make_async_copy(part, out_ref.at[source], done.at[k])
        for k, (part, source) in enumerate(zip(parts, sources))
    ]
    for copy in copies:
        copy.start()
    hits = known_ref[...] + odd_ref[...] + even_ref[...]
    lane = lax.broadcasted_iota(jnp.int32, hits.shape, 1)
    mine = jnp.where(lane == lax.axis_index("tile"), hits, 0.0)
    held_ref[...] = jnp.sum(mine[0:1], axis=1, keepdims=True) / RECV
    copies.append(pltpu.make_async_copy(held_ref, share_ref, done.at[groups]))
    copies[groups].start()
    listing.wait()
    for j in range(slots):
        list_ref[j] = blocks
    count = jnp.int32(0)
    for j in range(slots):
        block = named_ref[0, j]
        list_ref[count] = block
        count = count + jnp.where(block < blocks, 1, 0)

    def place(j):
        return pl.ds(pl.multiple_of(jnp.minimum(list_ref[j], blocks - 1) * BLK, BLK), BLK)

    def integrate(number):
        for j in range(number):
            for part, source in zip(parts, sources):
                rows = pl.ds(pl.multiple_of(source * species, species), species)
                picked_ref[rows, j * BLK : (j + 1) * BLK] = part[:, place(j)].astype(
                    jnp.float32
                )
        width = EACH * BLK
        spans = [slice(at, at + width) for at in range(0, number * BLK, width)]
        x = [picked_ref[:, span] for span in spans]
        hidden = [
            jnp.dot(w1_ref[...], v.astype(jnp.bfloat16), preferred_element_type=jnp.float32)
            for v in x
        ]
        hidden = [silu_of_half(v).astype(jnp.bfloat16) for v in hidden]
        hidden = [jnp.dot(w2_ref[...], v, preferred_element_type=jnp.float32) for v in hidden]
        hidden = [silu_of_half(v).astype(jnp.bfloat16) for v in hidden]
        for i, (v, h) in enumerate(zip(x, hidden)):
            v = v + jnp.dot(w3_ref[...], h, preferred_element_type=jnp.float32)
            for j in range(width // BLK):
                for g in range(groups):
                    fresh_ref[i * EACH + j, g] = v[
                        g * species : (g + 1) * species, j * BLK : (j + 1) * BLK
                    ].astype(jnp.bfloat16)

    for number in range(EACH, slots + 1, EACH):

        @pl.when((count > number - EACH) & (count <= number))
        def _():
            integrate(number)

    for copy in copies:
        copy.wait()

    def for_listed(act):
        for first in range(0, slots, EACH):

            @pl.when(first < count)
            def _():
                for j in range(first, first + EACH):

                    @pl.when(j < count)
                    def _():
                        act(
                            pltpu.make_async_copy(
                                fresh_ref.at[j], out_ref.at[:, :, place(j)], done.at[groups + 2 + j]
                            )
                        )

    for_listed(lambda copy: copy.start())
    for_listed(lambda copy: copy.wait())


def vmem():
    return pl.BlockSpec(memory_space=pltpu.VMEM)


def anywhere():
    return pl.BlockSpec(memory_space=pl.ANY)


def from_hbm(x):
    return pltpu.with_memory_space_constraint(x, pltpu.HBM)


def cost(us):
    return pl.CostEstimate(flops=int(us * 1e9), bytes_accessed=int(us * 3e6), transcendentals=0)


def shards(
    concentrations, courant, first_weight, middle_weight, last_weight, active_blocks, dest_tile
):
    species, length, cols = concentrations.shape
    dests = lax.axis_size("spec")
    tiles = lax.axis_size("tile")
    cells = length // dests * cols
    slots = active_blocks.shape[-1]
    halves = cols // LANES
    f32, bf16 = jnp.float32, jnp.bfloat16
    params = pltpu.CompilerParams(vmem_limit_bytes=VMEM_BYTES)
    size = halves * (BEHIND * species + SUB) + SUB
    flag = jax.ShapeDtypeStruct((SUB, LANES), f32)

    field, rates = tiled(concentrations, halves), tiled(courant, halves)
    to_even, to_odd, hits, listing = pl.pallas_call(
        functools.partial(pack_kernel, length, halves, cells // BLK),
        out_shape=[jax.ShapeDtypeStruct((size, LANES), f32)] * 2
        + [flag, jax.ShapeDtypeStruct((1, slots), jnp.int32)],
        in_specs=[anywhere()] * 5,
        out_specs=[vmem()] * 4,
        scratch_shapes=[
            pltpu.VMEM((species * halves * SUB, LANES), f32),
            pltpu.VMEM((species * halves * SUB, LANES), f32),
            pltpu.VMEM((2 * halves * SUB, LANES), f32),
            pltpu.SMEM((slots,), jnp.int32),
            pltpu.SMEM((slots,), jnp.int32),
            pltpu.SemaphoreType.DMA((7,)),
        ],
        compiler_params=params,
        cost_estimate=cost(1.0),
        name="pack_edges",
    )(
        from_hbm(field),
        from_hbm(rates),
        from_hbm(active_blocks.reshape(-1)),
        from_hbm(dest_tile.reshape(-1)),
        from_hbm(active_blocks.reshape(1, slots)),
    )
    field = field.reshape(species * length * halves, LANES)
    evens = [(t, t ^ 1) for t in range(tiles)]
    odds = [(t, ((t + 1) ^ 1) - 1) for t in range(tiles)]
    odds = [(t, other % tiles) for t, other in odds]
    from_odd = lax.ppermute(to_odd, "tile", odds)
    from_even = lax.ppermute(to_even, "tile", evens)
    block = jax.ShapeDtypeStruct((species, cells), bf16)
    blocks = pl.pallas_call(
        functools.partial(inner_kernel, dests, length, halves),
        out_shape=[block] * dests,
        in_specs=[vmem()] * 2,
        out_specs=[vmem()] * dests,
        compiler_params=params,
        cost_estimate=cost(1.0),
        name="inner_rows",
    )(field, rates)
    *blocks, to_even, to_odd, known = pl.pallas_call(
        functools.partial(edge_kernel, dests, length, halves),
        out_shape=[block] * dests + [flag] * 3,
        in_specs=[vmem()] * (5 + dests),
        out_specs=[vmem()] * (dests + 3),
        compiler_params=params,
        cost_estimate=cost(0.1),
        name="edge_rows",
    )(from_odd, from_even, hits, field, rates, *blocks)
    received = [blocks[0]] + [
        lax.ppermute(blocks[k], "spec", [(s, (s + k) % dests) for s in range(dests)])
        for k in range(1, dests)
    ]
    from_odd = lax.ppermute(to_odd, "tile", odds)
    from_even = lax.ppermute(to_even, "tile", evens)
    w1, w2 = pl.pallas_call(
        weight_kernel,
        out_shape=[jax.ShapeDtypeStruct(w.shape[::-1], bf16) for w in (first_weight, middle_weight)],
        in_specs=[vmem()] * 2 + [anywhere()],
        out_specs=[vmem()] * 2,
        compiler_params=params,
        cost_estimate=cost(0.5),
        name="halved_weights",
    )(first_weight, middle_weight, known)
    out, load_share = pl.pallas_call(
        functools.partial(chemistry_kernel, dests),
        out_shape=[
            jax.ShapeDtypeStruct((dests, species, cells), bf16),
            jax.ShapeDtypeStruct((1, 1), f32),
        ],
        in_specs=[anywhere()] + [vmem()] * (6 + dests),
        out_specs=[anywhere()] * 2,
        scratch_shapes=[
            pltpu.SMEM((1, slots), jnp.int32),
            pltpu.SMEM((slots + 1,), jnp.int32),
            pltpu.VMEM((dests * species, slots * BLK), f32),
            pltpu.VMEM((slots, dests, species, BLK), bf16),
            pltpu.VMEM((1, 1), f32),
            pltpu.SemaphoreType.DMA((dests + 2 + slots,)),
        ],
        compiler_params=params,
        cost_estimate=cost(4.0),
        name="chemistry",
    )(
        listing,
        w1,
        w2,
        last_weight.T,
        *received,
        known,
        from_odd,
        from_even,
    )
    return out.reshape(dests * species, cells), load_share


def solution(mesh):
    in_specs = (
        P("spec", "tile", None),
        P("tile", None),
        P(),
        P(),
        P(),
        P("tile", "spec", None),
        P("tile", "spec", None),
    )
    out_specs = (P(None, ("tile", "spec")), P("tile", "spec"))
    return jax.shard_map(shards, mesh=mesh, in_specs=in_specs, out_specs=out_specs, check_vma=False)
```

profile of v0, /device:TPU:0, one launch (start us, length us, event | category | flops | bytes accessed | tf_op | source)
XLA Modules:
  0.0 20.2 jit_solution(11345119515249808235)
XLA Ops:
  0.6 0.0 copy-start
  0.6 0.0 copy-start.1
  0.7 1.0 %pack_edges.1 = (f32[88,128]{1,0:T(8,128)S(1)}, f32[88,128]{1,0:T(8,128)S(1)}, f32[8,128]{1,0:T(8,128)S(1)}, s32[1,16]{1,0:T(1,128)S(1)}) custom-call(f32[8,128,128]{2,1,0:T(8,128)} %bitcast.17, f32[128,128]{1,0:T(8,128)} %bitcast.20, s32[16]{0:T(128)} %bitcast.24, s32[16]{0:T(128)} %bitcast.26, s32[1,16]{1,0:T(1,128)} %bitcast.25), custom_call_target="tpu_custom_call" | custom-call | flops 1000000000 | bytes 3000000 | tf_op jit(solution)/shard_map/pack_edges/pallas_call | solution.py:346
  1.7 3.4 %collective-permute-start = (f32[88,128]{1,0:T(8,128)S(1)}, f32[88,128]{1,0:T(8,128)S(1)}, u32[]{:S(2)}, u32[]{:S(2)}) collective-permute-start(f32[88,128]{1,0:T(8,128)S(1)} %get-tuple-element.22), channel_id=1, source_target_pairs={{0,28},{4,8},{8,4},{12,16},{16,12},{20,24},{24,20},{28,0},{1,29},{... | collective-permute-start | bytes 135176 | tf_op jit(solution)/shard_map/ppermute | solution.py:374
  5.1 0.0 collective-permute-start.1
  5.1 0.0 copy-done
  5.1 0.0 copy-done.1
  5.1 0.7 %inner_rows.1 = (bf16[8,4096]{1,0:T(8,128)(2,1)S(1)}, bf16[8,4096]{1,0:T(8,128)(2,1)S(1)}, bf16[8,4096]{1,0:T(8,128)(2,1)S(1)}, bf16[8,4096]{1,0:T(8,128)(2,1)S(1)}) custom-call(f32[1024,128]{1,0:T(8,128)S(1)} %bitcast.18, f32[128,128]{1,0:T(8,128)S(1)} %bitcast.21), custom_call_target="tpu_custom_call" | custom-call | flops 1000000000 | bytes 3000000 | tf_op jit(solution)/shard_map/inner_rows/pallas_call | solution.py:377
  5.8 0.0 copy-start.2
  5.8 1.0 %collective-permute-done.odd_ref = f32[88,128]{1,0:T(8,128)S(1)} collective-permute-done((f32[88,128]{1,0:T(8,128)S(1)}, f32[88,128]{1,0:T(8,128)S(1)}, u32[]{:S(2)}, u32[]{:S(2)}) %collective-permute-start) | collective-permute-done | bytes 45088 | tf_op jit(solution)/shard_map/ppermute | solution.py:374
  6.8 0.0 collective-permute-done.1.even_ref
  6.8 0.0 copy-start.3
  6.8 0.2 edge_rows.1
  7.0 2.8 %collective-permute-start.2 = (bf16[8,4096]{1,0:T(8,128)(2,1)S(1)}, bf16[8,4096]{1,0:T(8,128)(2,1)S(1)}, u32[]{:S(2)}, u32[]{:S(2)}) collective-permute-start(bf16[8,4096]{1,0:T(8,128)(2,1)S(1)} %get-tuple-element.33), channel_id=1, source_target_pairs={{0,1},{1,2},{2,3},{3,0},{4,5},{5,6},{6,7},{7,4},{8,9},{9,10},{10,1... | collective-permute-start | bytes 196616 | tf_op jit(solution)/shard_map/ppermute | solution.py:396
  9.7 2.6 %collective-permute-start.3 = (bf16[8,4096]{1,0:T(8,128)(2,1)S(1)}, bf16[8,4096]{1,0:T(8,128)(2,1)S(1)}, u32[]{:S(2)}, u32[]{:S(2)}) collective-permute-start(bf16[8,4096]{1,0:T(8,128)(2,1)S(1)} %get-tuple-element.34), channel_id=1, source_target_pairs={{0,2},{1,3},{2,0},{3,1},{4,6},{5,7},{6,4},{7,5},{8,10},{9,11},{10,... | collective-permute-start | bytes 196616 | tf_op jit(solution)/shard_map/ppermute | solution.py:396
  12.3 1.3 %collective-permute-start.4 = (bf16[8,4096]{1,0:T(8,128)(2,1)S(1)}, bf16[8,4096]{1,0:T(8,128)(2,1)S(1)}, u32[]{:S(2)}, u32[]{:S(2)}) collective-permute-start(bf16[8,4096]{1,0:T(8,128)(2,1)S(1)} %get-tuple-element.35), channel_id=1, source_target_pairs={{0,3},{1,0},{2,1},{3,2},{4,7},{5,4},{6,5},{7,6},{8,11},{9,8},{10,9... | collective-permute-start | bytes 196616 | tf_op jit(solution)/shard_map/ppermute | solution.py:396
  13.7 0.7 %collective-permute-start.5 = (f32[8,128]{1,0:T(8,128)S(1)}, f32[8,128]{1,0:T(8,128)S(1)}, u32[]{:S(2)}, u32[]{:S(2)}) collective-permute-start(f32[8,128]{1,0:T(8,128)S(1)} %get-tuple-element.36), channel_id=1, source_target_pairs={{0,28},{4,8},{8,4},{12,16},{16,12},{20,24},{24,20},{28,0},{1,29},{... | collective-permute-start | bytes 12296 | tf_op jit(solution)/shard_map/ppermute | solution.py:399
  14.3 0.0 collective-permute-start.6
  14.3 0.0 copy-done.2
  14.3 0.0 copy-done.3
  14.4 0.0 copy-start.4
  14.4 0.2 %halved_weights.1 = (bf16[512,32]{1,0:T(8,128)(2,1)S(1)}, bf16[512,512]{1,0:T(8,128)(2,1)S(1)}) custom-call(bf16[32,512]{1,0:T(8,128)(2,1)S(1)} %copy-done.3, bf16[512,512]{1,0:T(8,128)(2,1)S(1)} %copy-done.2, f32[8,128]{1,0:T(8,128)S(1)} %get-tuple-element.29.after_ref.refs_4_), custom_call_target="tpu_custom_call" | custom-call | flops 500000000 | bytes 1500000 | tf_op jit(solution)/shard_map/halved_weights/pallas_call | solution.py:401
  14.6 3.0 %collective-permute-done.5.refs_5_ = f32[8,128]{1,0:T(8,128)S(1)} collective-permute-done((f32[8,128]{1,0:T(8,128)S(1)}, f32[8,128]{1,0:T(8,128)S(1)}, u32[]{:S(2)}, u32[]{:S(2)}) %collective-permute-start.5) | collective-permute-done | bytes 4128 | tf_op jit(solution)/shard_map/ppermute | solution.py:399
  17.6 0.0 collective-permute-done.6.refs_6_
  17.6 0.0 collective-permute-done.2.refs_1_
  17.6 0.0 collective-permute-done.3.refs_2_
  17.6 0.0 collective-permute-done.4.refs_3_
  17.6 0.0 copy-done.4
  17.6 2.6 %chemistry.1 = (bf16[4,8,4096]{2,1,0:T(8,128)(2,1)}, f32[1,1]{1,0:T(1,128)}) custom-call(s32[1,16]{1,0:T(1,128)S(1)} %get-tuple-element.21.named_in, bf16[512,32]{1,0:T(8,128)(2,1)S(1)} %get-tuple-element.30.w1_ref, bf16[512,512]{1,0:T(8,128)(2,1)S(1)} %get-tuple-element.31.w2_ref, bf16[32,512]{1,0:T(8,128)(2,1)S(1)} %bitcast.23, ...), custom_call_target="tpu_custom_call" | custom-call | flops 4000000000 | bytes 12000000 | tf_op jit(solution)/shard_map/chemistry/pallas_call | solution.py:410
Async XLA Ops:
  0.6 4.5 %copy-start = (f32[8,64,256]{2,1,0:T(8,128)S(1)}, f32[8,64,256]{2,1,0:T(8,128)}, u32[]{:S(2)}) copy-start(f32[8,64,256]{2,1,0:T(8,128)} %param.7) | copy-start | bytes 1572868
  0.6 4.4 %copy-start.1 = (f32[64,256]{1,0:T(8,128)S(1)}, f32[64,256]{1,0:T(8,128)}, u32[]{:S(2)}) copy-start(f32[64,256]{1,0:T(8,128)} %param.8) | copy-start | bytes 196612
  1.7 5.1 %collective-permute-start = (f32[88,128]{1,0:T(8,128)S(1)}, f32[88,128]{1,0:T(8,128)S(1)}, u32[]{:S(2)}, u32[]{:S(2)}) collective-permute-start(f32[88,128]{1,0:T(8,128)S(1)} %get-tuple-element.22), channel_id=1, source_target_pairs={{0,28},{4,8},{8,4},{12,16},{16,12},{20,24},{24,20},{28,0},{1,29},{... | collective-permute-start | bytes 135176 | tf_op jit(solution)/shard_map/ppermute | solution.py:374
  5.1 1.7 %collective-permute-start.1 = (f32[88,128]{1,0:T(8,128)S(1)}, f32[88,128]{1,0:T(8,128)S(1)}, u32[]{:S(2)}, u32[]{:S(2)}) collective-permute-start(f32[88,128]{1,0:T(8,128)S(1)} %get-tuple-element.23), channel_id=1, source_target_pairs={{0,4},{4,0},{8,12},{12,8},{16,20},{20,16},{24,28},{28,24},{1,5},{5... | collective-permute-start | bytes 135176 | tf_op jit(solution)/shard_map/ppermute | solution.py:375
  5.8 8.6 %copy-start.2 = (bf16[512,512]{1,0:T(8,128)(2,1)S(1)}, bf16[512,512]{1,0:T(8,128)(2,1)}, u32[]{:S(2)}) copy-start(bf16[512,512]{1,0:T(8,128)(2,1)} %w2_ref.1) | copy-start | bytes 1572868
  6.8 7.5 %copy-start.3 = (bf16[32,512]{1,0:T(8,128)(2,1)S(1)}, bf16[32,512]{1,0:T(8,128)(2,1)}, u32[]{:S(2)}) copy-start(bf16[32,512]{1,0:T(8,128)(2,1)} %w1_ref.1) | copy-start | bytes 98308
  7.0 10.6 %collective-permute-start.2 = (bf16[8,4096]{1,0:T(8,128)(2,1)S(1)}, bf16[8,4096]{1,0:T(8,128)(2,1)S(1)}, u32[]{:S(2)}, u32[]{:S(2)}) collective-permute-start(bf16[8,4096]{1,0:T(8,128)(2,1)S(1)} %get-tuple-element.33), channel_id=1, source_target_pairs={{0,1},{1,2},{2,3},{3,0},{4,5},{5,6},{6,7},{7,4},{8,9},{9,10},{10,1... | collective-permute-start | bytes 196616 | tf_op jit(solution)/shard_map/ppermute | solution.py:396
  9.7 7.9 %collective-permute-start.3 = (bf16[8,4096]{1,0:T(8,128)(2,1)S(1)}, bf16[8,4096]{1,0:T(8,128)(2,1)S(1)}, u32[]{:S(2)}, u32[]{:S(2)}) collective-permute-start(bf16[8,4096]{1,0:T(8,128)(2,1)S(1)} %get-tuple-element.34), channel_id=1, source_target_pairs={{0,2},{1,3},{2,0},{3,1},{4,6},{5,7},{6,4},{7,5},{8,10},{9,11},{10,... | collective-permute-start | bytes 196616 | tf_op jit(solution)/shard_map/ppermute | solution.py:396
  12.3 5.3 %collective-permute-start.4 = (bf16[8,4096]{1,0:T(8,128)(2,1)S(1)}, bf16[8,4096]{1,0:T(8,128)(2,1)S(1)}, u32[]{:S(2)}, u32[]{:S(2)}) collective-permute-start(bf16[8,4096]{1,0:T(8,128)(2,1)S(1)} %get-tuple-element.35), channel_id=1, source_target_pairs={{0,3},{1,0},{2,1},{3,2},{4,7},{5,4},{6,5},{7,6},{8,11},{9,8},{10,9... | collective-permute-start | bytes 196616 | tf_op jit(solution)/shard_map/ppermute | solution.py:396
  13.7 3.9 %collective-permute-start.5 = (f32[8,128]{1,0:T(8,128)S(1)}, f32[8,128]{1,0:T(8,128)S(1)}, u32[]{:S(2)}, u32[]{:S(2)}) collective-permute-start(f32[8,128]{1,0:T(8,128)S(1)} %get-tuple-element.36), channel_id=1, source_target_pairs={{0,28},{4,8},{8,4},{12,16},{16,12},{20,24},{24,20},{28,0},{1,29},{... | collective-permute-start | bytes 12296 | tf_op jit(solution)/shard_map/ppermute | solution.py:399
  14.3 3.3 %collective-permute-start.6 = (f32[8,128]{1,0:T(8,128)S(1)}, f32[8,128]{1,0:T(8,128)S(1)}, u32[]{:S(2)}, u32[]{:S(2)}) collective-permute-start(f32[8,128]{1,0:T(8,128)S(1)} %get-tuple-element.37), channel_id=1, source_target_pairs={{0,4},{4,0},{8,12},{12,8},{16,20},{20,16},{24,28},{28,24},{1,5},{5... | collective-permute-start | bytes 12296 | tf_op jit(solution)/shard_map/ppermute | solution.py:400
  14.4 3.3 %copy-start.4 = (bf16[512,32]{0,1:T(8,128)(2,1)S(1)}, bf16[512,32]{0,1:T(8,128)(2,1)}, u32[]{:S(2)}) copy-start(bf16[512,32]{0,1:T(8,128)(2,1)} %param.11) | copy-start | bytes 98308
where the time goes:
time: 20.6 us; the launch traced here: 20.2 us
  starting transfers between devices  10.8 us (52%)
  Pallas kernels  4.7 us (23%)
  waiting for transfers between devices  4.02 us (20%)
  between operations  0.73 us (4%)
    ppermute x3, starting transfers between devices, shards(): lax.ppermute(blocks[k], 'spec', [(s, (s + k) % dests) for s in range(dest...  6.7 us
    ppermute x2, starting transfers between devices, shards(): from_odd = lax.ppermute(to_odd, 'tile', odds)  4.07 us
    ppermute x2, waiting for transfers between devices, shards(): from_odd = lax.ppermute(to_odd, 'tile', odds)  4 us
    pallas_call x1, Pallas kernels, shards(): pl.pallas_call(functools.partial(chemistry_kernel, dests), out_shape=[jax...  2.59 us
    pallas_call x1, Pallas kernels, shards(): pl.pallas_call(functools.partial(pack_kernel, length, halves, cells // BL...  1.02 us
    pallas_call x1, Pallas kernels, shards(): pl.pallas_call(functools.partial(inner_kernel, dests, length, halves), ou...  0.69 us
  transfers between devices with their start and end apart: 7, of which 2 were waited for; matrix products, arithmetic and copies ran while one was open for 0% of the time, Pallas kernels for 5%

commit v1 on v0

--- a/solution.py
+++ b/solution.py
@@ -221,6 +221,10 @@
     w2_out[...] = (0.5 * w2_ref[...].astype(jnp.float32)).T.astype(jnp.bfloat16)
 
 
+def ring_order(count):
+    return [0, 1] + list(range(count - 1, 1, -1))
+
+
 def chemistry_kernel(
     groups, named_in, w1_ref, w2_ref, w3_ref, *refs
 ):
@@ -234,7 +238,7 @@
     slots = named_ref.shape[1]
     blocks = cells // BLK
     me = lax.axis_index("spec")
-    sources = [lax.rem(me - k + groups, groups) for k in range(groups)]
+    sources = [lax.rem(me - k + groups, groups) for k in ring_order(groups)]
     copies = [
         pltpu.make_async_copy(part, out_ref.at[source], done.at[k])
         for k, (part, source) in enumerate(zip(parts, sources))
@@ -431,7 +435,7 @@
         w1,
         w2,
         last_weight.T,
-        *received,
+        *[received[k] for k in ring_order(dests)],
         known,
         from_odd,
         from_even,

time: 20.6 us -> 20.3 us (0.985); the launches traced: 20.2 us -> 20.2 us
  starting transfers between devices: 10.8 us -> 9.87 us
  waiting for transfers between devices: 4.02 us -> 4.87 us
    ppermute x3, starting transfers between devices: 6.7 us -> 5.8 us  [shards(): lax.ppermute(blocks[k], 'spec', [(s, (s + k) % dests) for s in range(dest...]
    ppermute x3, waiting for transfers between devices: 0.01 us -> 0.86 us  [shards(): lax.ppermute(blocks[k], 'spec', [(s, (s + k) % dests) for s in range(dest...]
  transfers between devices with their start and end apart: 7 -> 7, of which waited for: 2 -> 3; matrix products, arithmetic and copies ran while one was open for 0% -> 0% of each run, Pallas kernels for 5% -> 5%
where the time goes in v1:
time: 20.3 us; the launch traced here: 20.2 us
  starting transfers between devices  9.87 us (49%)
  waiting for transfers between devices  4.87 us (24%)
  Pallas kernels  4.68 us (23%)
  between operations  0.71 us (3%)
    ppermute x3, starting transfers between devices, shards(): lax.ppermute(blocks[k], 'spec', [(s, (s + k) % dests) for s in range(dest...  5.8 us
    ppermute x2, starting transfers between devices, shards(): from_odd = lax.ppermute(to_odd, 'tile', odds)  4.07 us
    ppermute x2, waiting for transfers between devices, shards(): from_odd = lax.ppermute(to_odd, 'tile', odds)  4 us
    pallas_call x1, Pallas kernels, shards(): pl.pallas_call(functools.partial(chemistry_kernel, dests), out_shape=[jax...  2.58 us
    pallas_call x1, Pallas kernels, shards(): pl.pallas_call(functools.partial(pack_kernel, length, halves, cells // BL...  1.02 us
    ppermute x3, waiting for transfers between devices, shards(): lax.ppermute(blocks[k], 'spec', [(s, (s + k) % dests) for s in range(dest...  0.86 us
    pallas_call x1, Pallas kernels, shards(): pl.pallas_call(functools.partial(inner_kernel, dests, length, halves), ou...  0.69 us
  transfers between devices with their start and end apart: 7, of which 3 were waited for; matrix products, arithmetic and copies ran while one was open for 0% of the time, Pallas kernels for 5%

profile of v1, /device:TPU:0, one launch (start us, length us, event | category | flops | bytes accessed | tf_op | source)
XLA Modules:
  0.0 20.2 jit_solution(11739537635655764114)
XLA Ops:
  0.6 0.0 copy-start
  0.6 0.0 copy-start.1
  0.7 1.0 %pack_edges.1 = (f32[88,128]{1,0:T(8,128)S(1)}, f32[88,128]{1,0:T(8,128)S(1)}, f32[8,128]{1,0:T(8,128)S(1)}, s32[1,16]{1,0:T(1,128)S(1)}) custom-call(f32[8,128,128]{2,1,0:T(8,128)} %bitcast.17, f32[128,128]{1,0:T(8,128)} %bitcast.20, s32[16]{0:T(128)} %bitcast.24, s32[16]{0:T(128)} %bitcast.26, s32[1,16]{1,0:T(1,128)} %bitcast.25), custom_call_target="tpu_custom_call" | custom-call | flops 1000000000 | bytes 3000000 | tf_op jit(solution)/shard_map/pack_edges/pallas_call | solution.py:350
  1.7 3.4 %collective-permute-start = (f32[88,128]{1,0:T(8,128)S(1)}, f32[88,128]{1,0:T(8,128)S(1)}, u32[]{:S(2)}, u32[]{:S(2)}) collective-permute-start(f32[88,128]{1,0:T(8,128)S(1)} %get-tuple-element.22), channel_id=1, source_target_pairs={{0,28},{4,8},{8,4},{12,16},{16,12},{20,24},{24,20},{28,0},{1,29},{... | collective-permute-start | bytes 135176 | tf_op jit(solution)/shard_map/ppermute | solution.py:378
  5.1 0.0 collective-permute-start.1
  5.1 0.0 copy-done
  5.1 0.0 copy-done.1
  5.1 0.7 %inner_rows.1 = (bf16[8,4096]{1,0:T(8,128)(2,1)S(1)}, bf16[8,4096]{1,0:T(8,128)(2,1)S(1)}, bf16[8,4096]{1,0:T(8,128)(2,1)S(1)}, bf16[8,4096]{1,0:T(8,128)(2,1)S(1)}) custom-call(f32[1024,128]{1,0:T(8,128)S(1)} %bitcast.18, f32[128,128]{1,0:T(8,128)S(1)} %bitcast.21), custom_call_target="tpu_custom_call" | custom-call | flops 1000000000 | bytes 3000000 | tf_op jit(solution)/shard_map/inner_rows/pallas_call | solution.py:381
  5.8 0.0 copy-start.2
  5.8 1.0 %collective-permute-done.odd_ref = f32[88,128]{1,0:T(8,128)S(1)} collective-permute-done((f32[88,128]{1,0:T(8,128)S(1)}, f32[88,128]{1,0:T(8,128)S(1)}, u32[]{:S(2)}, u32[]{:S(2)}) %collective-permute-start) | collective-permute-done | bytes 45088 | tf_op jit(solution)/shard_map/ppermute | solution.py:378
  6.8 0.0 collective-permute-done.1.even_ref
  6.8 0.0 copy-start.3
  6.8 0.2 edge_rows.1
  7.0 2.8 %collective-permute-start.2 = (bf16[8,4096]{1,0:T(8,128)(2,1)S(1)}, bf16[8,4096]{1,0:T(8,128)(2,1)S(1)}, u32[]{:S(2)}, u32[]{:S(2)}) collective-permute-start(bf16[8,4096]{1,0:T(8,128)(2,1)S(1)} %get-tuple-element.33), channel_id=1, source_target_pairs={{0,1},{1,2},{2,3},{3,0},{4,5},{5,6},{6,7},{7,4},{8,9},{9,10},{10,1... | collective-permute-start | bytes 196616 | tf_op jit(solution)/shard_map/ppermute | solution.py:400
  9.7 2.1 %collective-permute-start.3 = (bf16[8,4096]{1,0:T(8,128)(2,1)S(1)}, bf16[8,4096]{1,0:T(8,128)(2,1)S(1)}, u32[]{:S(2)}, u32[]{:S(2)}) collective-permute-start(bf16[8,4096]{1,0:T(8,128)(2,1)S(1)} %get-tuple-element.34), channel_id=1, source_target_pairs={{0,3},{1,0},{2,1},{3,2},{4,7},{5,4},{6,5},{7,6},{8,11},{9,8},{10,9... | collective-permute-start | bytes 196616 | tf_op jit(solution)/shard_map/ppermute | solution.py:400
  11.8 0.9 %collective-permute-start.4 = (bf16[8,4096]{1,0:T(8,128)(2,1)S(1)}, bf16[8,4096]{1,0:T(8,128)(2,1)S(1)}, u32[]{:S(2)}, u32[]{:S(2)}) collective-permute-start(bf16[8,4096]{1,0:T(8,128)(2,1)S(1)} %get-tuple-element.35), channel_id=1, source_target_pairs={{0,2},{1,3},{2,0},{3,1},{4,6},{5,7},{6,4},{7,5},{8,10},{9,11},{10,... | collective-permute-start | bytes 196616 | tf_op jit(solution)/shard_map/ppermute | solution.py:400
  12.8 0.7 %collective-permute-start.5 = (f32[8,128]{1,0:T(8,128)S(1)}, f32[8,128]{1,0:T(8,128)S(1)}, u32[]{:S(2)}, u32[]{:S(2)}) collective-permute-start(f32[8,128]{1,0:T(8,128)S(1)} %get-tuple-element.36), channel_id=1, source_target_pairs={{0,28},{4,8},{8,4},{12,16},{16,12},{20,24},{24,20},{28,0},{1,29},{... | collective-permute-start | bytes 12296 | tf_op jit(solution)/shard_map/ppermute | solution.py:403
  13.4 0.0 collective-permute-start.6
  13.4 0.0 copy-done.2
  13.5 0.0 copy-done.3
  13.5 0.0 copy-start.4
  13.5 0.2 %halved_weights.1 = (bf16[512,32]{1,0:T(8,128)(2,1)S(1)}, bf16[512,512]{1,0:T(8,128)(2,1)S(1)}) custom-call(bf16[32,512]{1,0:T(8,128)(2,1)S(1)} %copy-done.3, bf16[512,512]{1,0:T(8,128)(2,1)S(1)} %copy-done.2, f32[8,128]{1,0:T(8,128)S(1)} %get-tuple-element.29.after_ref.refs_4_), custom_call_target="tpu_custom_call" | custom-call | flops 500000000 | bytes 1500000 | tf_op jit(solution)/shard_map/halved_weights/pallas_call | solution.py:405
  13.7 3.0 %collective-permute-done.5.refs_5_ = f32[8,128]{1,0:T(8,128)S(1)} collective-permute-done((f32[8,128]{1,0:T(8,128)S(1)}, f32[8,128]{1,0:T(8,128)S(1)}, u32[]{:S(2)}, u32[]{:S(2)}) %collective-permute-start.5) | collective-permute-done | bytes 4128 | tf_op jit(solution)/shard_map/ppermute | solution.py:403
  16.7 0.0 collective-permute-done.6.refs_6_
  16.7 0.0 collective-permute-done.2.refs_1_
  16.7 0.0 collective-permute-done.3.refs_2_
  16.7 0.9 %collective-permute-done.4.refs_3_ = bf16[8,4096]{1,0:T(8,128)(2,1)S(1)} collective-permute-done((bf16[8,4096]{1,0:T(8,128)(2,1)S(1)}, bf16[8,4096]{1,0:T(8,128)(2,1)S(1)}, u32[]{:S(2)}, u32[]{:S(2)}) %collective-permute-start.4) | collective-permute-done | bytes 65568 | tf_op jit(solution)/shard_map/ppermute | solution.py:400
  17.6 0.0 copy-done.4
  17.6 2.6 %chemistry.1 = (bf16[4,8,4096]{2,1,0:T(8,128)(2,1)}, f32[1,1]{1,0:T(1,128)}) custom-call(s32[1,16]{1,0:T(1,128)S(1)} %get-tuple-element.21.named_in, bf16[512,32]{1,0:T(8,128)(2,1)S(1)} %get-tuple-element.30.w1_ref, bf16[512,512]{1,0:T(8,128)(2,1)S(1)} %get-tuple-element.31.w2_ref, bf16[32,512]{1,0:T(8,128)(2,1)S(1)} %bitcast.23, ...), custom_call_target="tpu_custom_call" | custom-call | flops 4000000000 | bytes 12000000 | tf_op jit(solution)/shard_map/chemistry/pallas_call | solution.py:414
Async XLA Ops:
  0.6 4.5 %copy-start = (f32[8,64,256]{2,1,0:T(8,128)S(1)}, f32[8,64,256]{2,1,0:T(8,128)}, u32[]{:S(2)}) copy-start(f32[8,64,256]{2,1,0:T(8,128)} %param.7) | copy-start | bytes 1572868
  0.6 4.4 %copy-start.1 = (f32[64,256]{1,0:T(8,128)S(1)}, f32[64,256]{1,0:T(8,128)}, u32[]{:S(2)}) copy-start(f32[64,256]{1,0:T(8,128)} %param.8) | copy-start | bytes 196612
  1.7 5.1 %collective-permute-start = (f32[88,128]{1,0:T(8,128)S(1)}, f32[88,128]{1,0:T(8,128)S(1)}, u32[]{:S(2)}, u32[]{:S(2)}) collective-permute-start(f32[88,128]{1,0:T(8,128)S(1)} %get-tuple-element.22), channel_id=1, source_target_pairs={{0,28},{4,8},{8,4},{12,16},{16,12},{20,24},{24,20},{28,0},{1,29},{... | collective-permute-start | bytes 135176 | tf_op jit(solution)/shard_map/ppermute | solution.py:378
  5.1 1.7 %collective-permute-start.1 = (f32[88,128]{1,0:T(8,128)S(1)}, f32[88,128]{1,0:T(8,128)S(1)}, u32[]{:S(2)}, u32[]{:S(2)}) collective-permute-start(f32[88,128]{1,0:T(8,128)S(1)} %get-tuple-element.23), channel_id=1, source_target_pairs={{0,4},{4,0},{8,12},{12,8},{16,20},{20,16},{24,28},{28,24},{1,5},{5... | collective-permute-start | bytes 135176 | tf_op jit(solution)/shard_map/ppermute | solution.py:379
  5.8 7.7 %copy-start.2 = (bf16[512,512]{1,0:T(8,128)(2,1)S(1)}, bf16[512,512]{1,0:T(8,128)(2,1)}, u32[]{:S(2)}) copy-start(bf16[512,512]{1,0:T(8,128)(2,1)} %w2_ref.1) | copy-start | bytes 1572868
  6.8 6.6 %copy-start.3 = (bf16[32,512]{1,0:T(8,128)(2,1)S(1)}, bf16[32,512]{1,0:T(8,128)(2,1)}, u32[]{:S(2)}) copy-start(bf16[32,512]{1,0:T(8,128)(2,1)} %w1_ref.1) | copy-start | bytes 98308
  7.0 9.7 %collective-permute-start.2 = (bf16[8,4096]{1,0:T(8,128)(2,1)S(1)}, bf16[8,4096]{1,0:T(8,128)(2,1)S(1)}, u32[]{:S(2)}, u32[]{:S(2)}) collective-permute-start(bf16[8,4096]{1,0:T(8,128)(2,1)S(1)} %get-tuple-element.33), channel_id=1, source_target_pairs={{0,1},{1,2},{2,3},{3,0},{4,5},{5,6},{6,7},{7,4},{8,9},{9,10},{10,1... | collective-permute-start | bytes 196616 | tf_op jit(solution)/shard_map/ppermute | solution.py:400
  9.7 7.0 %collective-permute-start.3 = (bf16[8,4096]{1,0:T(8,128)(2,1)S(1)}, bf16[8,4096]{1,0:T(8,128)(2,1)S(1)}, u32[]{:S(2)}, u32[]{:S(2)}) collective-permute-start(bf16[8,4096]{1,0:T(8,128)(2,1)S(1)} %get-tuple-element.34), channel_id=1, source_target_pairs={{0,3},{1,0},{2,1},{3,2},{4,7},{5,4},{6,5},{7,6},{8,11},{9,8},{10,9... | collective-permute-start | bytes 196616 | tf_op jit(solution)/shard_map/ppermute | solution.py:400
  11.8 5.8 %collective-permute-start.4 = (bf16[8,4096]{1,0:T(8,128)(2,1)S(1)}, bf16[8,4096]{1,0:T(8,128)(2,1)S(1)}, u32[]{:S(2)}, u32[]{:S(2)}) collective-permute-start(bf16[8,4096]{1,0:T(8,128)(2,1)S(1)} %get-tuple-element.35), channel_id=1, source_target_pairs={{0,2},{1,3},{2,0},{3,1},{4,6},{5,7},{6,4},{7,5},{8,10},{9,11},{10,... | collective-permute-start | bytes 196616 | tf_op jit(solution)/shard_map/ppermute | solution.py:400
  12.8 3.9 %collective-permute-start.5 = (f32[8,128]{1,0:T(8,128)S(1)}, f32[8,128]{1,0:T(8,128)S(1)}, u32[]{:S(2)}, u32[]{:S(2)}) collective-permute-start(f32[8,128]{1,0:T(8,128)S(1)} %get-tuple-element.36), channel_id=1, source_target_pairs={{0,28},{4,8},{8,4},{12,16},{16,12},{20,24},{24,20},{28,0},{1,29},{... | collective-permute-start | bytes 12296 | tf_op jit(solution)/shard_map/ppermute | solution.py:403
  13.4 3.3 %collective-permute-start.6 = (f32[8,128]{1,0:T(8,128)S(1)}, f32[8,128]{1,0:T(8,128)S(1)}, u32[]{:S(2)}, u32[]{:S(2)}) collective-permute-start(f32[8,128]{1,0:T(8,128)S(1)} %get-tuple-element.37), channel_id=1, source_target_pairs={{0,4},{4,0},{8,12},{12,8},{16,20},{20,16},{24,28},{28,24},{1,5},{5... | collective-permute-start | bytes 12296 | tf_op jit(solution)/shard_map/ppermute | solution.py:404
  13.5 4.1 %copy-start.4 = (bf16[512,32]{0,1:T(8,128)(2,1)S(1)}, bf16[512,32]{0,1:T(8,128)(2,1)}, u32[]{:S(2)}) copy-start(bf16[512,32]{0,1:T(8,128)(2,1)} %param.11) | copy-start | bytes 98308
